TPU v7x, 32 devices: a whole 2x2x4 slice. The times are simulated.
32 devices in a mesh: row: 8 (over z, x), col: 4 (over y, core).
Axes of the slice: x: 2, y: 2, z: 4, core: 2. Of those that a mesh axis runs over, the one named last changes fastest.
Arguments:
- gradient: bfloat16 [8192, 28672], P('row', 'col'), may hold values from -6 to 6
- projector: bfloat16 [8192, 1024], P('row'), may hold values from -0.25 to 0.25
- first_moment: float32 [1024, 28672], P('row', 'col'), may hold values from -6 to 6
- second_moment: float32 [1024, 28672], P('row', 'col'), may hold values from 5e-05 to 0.12, as said below
Outputs:
- update: bfloat16 [8192, 28672], P('row', 'col')
- first_new: float32 [1024, 28672], P('row', 'col')
- second_new: float32 [1024, 28672], P('row', 'col')
Inputs may be any that keep to these rules, and one draw needn't show every extreme that they name: `second_moment`: entries are positive.
All inputs are finite; a program needn't handle non-finite values.
Results may differ from a plain program's by a relative error of at most 0.038.
Values may be sent and summed in bfloat16 or wider, within the bound.
A program may use at most 128 MiB of HBM per device.

v0:
```python
import jax
import jax.numpy as jnp
from jax import lax
from jax.sharding import PartitionSpec as P

FF = 28672
R = 1024


decay_first = 0.9
decay_second = 0.999
bias_first = 1.0 - 0.9**10
bias_second = 1.0 - 0.999**10
epsilon = 1e-08
clip_limit = 0.5


def local(gradient, projector, first_moment, second_moment):
    chosen = projector
    product = lax.dot_general(
        chosen, gradient, (((0,), (0,)), ((), ())), preferred_element_type=jnp.float32
    )
    rounded = lax.optimization_barrier(product.astype(jnp.bfloat16))
    lowrank = lax.psum_scatter(
        rounded.astype(jnp.float32).astype(jnp.bfloat16), "row", scatter_dimension=0, tiled=True
    ).astype(jnp.float32)
    first_new = decay_first * first_moment + (1.0 - decay_first) * lowrank
    second_new = decay_second * second_moment + (1.0 - decay_second) * lowrank * lowrank
    direction = first_new / bias_first / (jnp.sqrt(second_new / bias_second) + epsilon)
    square_total = jnp.sum(direction * direction)
    total = lax.psum(square_total, ("row", "col"))
    root_mean = jnp.sqrt(total / (R * FF) + 1e-06)
    factor = jnp.minimum(1.0, clip_limit / root_mean)
    step_low = (factor * direction).astype(jnp.bfloat16)
    chosen = projector
    projected = jnp.dot(
        chosen,
        lax.all_gather(step_low, "row", axis=0, tiled=True),
        preferred_element_type=jnp.float32,
    )
    updates = projected.astype(jnp.bfloat16)
    return (updates, first_new, second_new)


def solution(mesh):
    placed = (P("row", "col"), P("row", None), P("row", "col"), P("row", "col"))
    return jax.shard_map(
        local,
        mesh=mesh,
        in_specs=placed,
        out_specs=(P("row", "col"), P("row", "col"), P("row", "col")),
        check_vma=False,
    )
```

profile of v0, /device:TPU:0, one launch (start us, length us, event | category | flops | bytes accessed | tf_op | source)
XLA Modules:
  0.0 578.2 jit_solution(15425990916094827354)
XLA Ops:
  7.2 0.0 copy-start
  7.2 0.0 reduce-scatter.2.cloned.1.call-start
  7.2 1.5 copy-done
  8.8 23.2 %convolution_convert_fusion = bf16[1024,7168]{1,0:T(8,128)(2,1)} fusion(bf16[1024,1024]{1,0:T(8,128)(2,1)S(1)} %copy-done, bf16[1024,7168]{1,0:T(8,128)(2,1)} %param.4), kind=kOutput, calls=%fused_computation.1 | convolution fusion | flops 15039725568 | bytes 31457280 | tf_op jit(solution)/shard_map/dot_general | solution.py:20
  32.0 0.0 reduce-scatter.2.cloned.1.call-update
  32.0 0.0 all-gather.2.cloned.1.call-start
  32.1 239.3 %reduce-scatter.2.cloned.1.call-done = bf16[128,7168]{1,0:T(8,128)(2,1)} async-done(((bf16[1024,7168]{1,0:T(8,128)(2,1)}), bf16[128,7168]{1,0:T(8,128)(2,1)}) %reduce-scatter.2.cloned.1.call-update) | async-done | bytes 1835024 | tf_op jit(solution)/shard_map/reduce_scatter | solution.py:24
  271.4 7.4 %multiply_reduce_fusion = (f32[]{:T(128)}, f32[128,7168]{1,0:T(8,128)}, f32[128,7168]{1,0:T(8,128)}) fusion(bf16[128,7168]{1,0:T(8,128)(2,1)} %reduce-scatter.2.cloned.1.call-done, f32[128,7168]{1,0:T(8,128)} %param.6, f32[128,7168]{1,0:T(8,128)} %param.7), kind=kLoop, calls=%fused_computation.7 | loop fusion | flops 12845055 | bytes 16515076 | tf_op jit(solution)/shard_map/reduce_sum | solution.py:30
  278.8 39.7 %psum.7 = f32[]{:T(128)} all-reduce(f32[]{:T(128)} %get-tuple-element.6), channel_id=1, replica_groups=mesh['row'=8,'col'=4] {'row','col'}, use_global_device_ids=true, to_apply=%region_2.0 | all-reduce | flops 1 | bytes 8 | tf_op jit(solution)/shard_map/psum | solution.py:31
  319.2 6.0 %multiply_convert_fusion = bf16[128,7168]{1,0:T(8,128)(2,1)} fusion(f32[]{:T(128)S(6)} %min_shard_map.3, f32[128,7168]{1,0:T(8,128)} %get-tuple-element.8, f32[128,7168]{1,0:T(8,128)} %get-tuple-element.7), kind=kLoop, calls=%fused_computation.6 | loop fusion | flops 5505024 | bytes 9175044 | tf_op jit(solution)/shard_map/convert_element_type | solution.py:34
  325.2 0.0 all-gather.2.cloned.1.call-update
  325.3 202.1 %all-gather.2.cloned.1.call-done = bf16[1024,7168]{1,0:T(8,128)(2,1)} async-done(((bf16[128,7168]{1,0:T(8,128)(2,1)}), bf16[1024,7168]{1,0:T(8,128)(2,1)}) %all-gather.2.cloned.1.call-update) | async-done | bytes 14680080 | tf_op jit(solution)/shard_map/all_gather | solution.py:38
  527.4 23.9 %convert_bitcast_fusion = bf16[1024,7168]{0,1:T(8,128)(2,1)} fusion(bf16[1024,7168]{1,0:T(8,128)(2,1)} %all-gather.2.cloned.1.call-done, bf16[1024,1024]{1,0:T(8,128)(2,1)S(1)} %copy-done), kind=kOutput, calls=%fused_computation | convolution fusion | flops 15039725568 | bytes 31457280 | tf_op jit(solution)/shard_map/dot_general | solution.py:36
  551.3 0.0 copy-start.1
  551.3 20.1 %copy.7 = bf16[1024,7168]{1,0:T(8,128)(2,1)} copy(bf16[1024,7168]{0,1:T(8,128)(2,1)} %convert_bitcast_fusion) | data formatting | bytes 29360128
  571.3 0.0 copy-done.1
Async XLA Ops:
  7.2 1.6 copy-start
  7.2 264.2 %reduce-scatter.2.cloned.1.call-start = ((), (), s32[]{:S(2)}) async-start(), calls=%async_computation.1 | async-start | bytes 16515072 | tf_op jit(solution)/shard_map/reduce_scatter | solution.py:24
  32.0 495.4 %all-gather.2.cloned.1.call-start = ((), (), s32[]{:S(2)}) async-start(), calls=%async_computation.2 | async-start | bytes 16515072 | tf_op jit(solution)/shard_map/all_gather | solution.py:38
  551.3 20.1 %copy-start.1 = (bf16[1024,1024]{1,0:T(8,128)(2,1)S(1)}, bf16[1024,1024]{1,0:T(8,128)(2,1)}, u32[]{:S(2)}) copy-start(bf16[1024,1024]{1,0:T(8,128)(2,1)} %param.5) | copy-start | bytes 6291460
Sparse Core Ops, SparseCore 0:
  32.1 239.2 reduce-scatter.1
  325.4 201.9 all-gather.1
where the time goes:
time: 579 us; the launch traced here: 578 us
  waiting for transfers between devices  442 us (76%)
  matrix products  47.1 us (8%)
  blocking collectives  39.7 us (7%)
  local copies, waits for them, and re-layouts  21.6 us (4%)
  between operations  14.7 us (3%)
  other arithmetic  13.4 us (2%)
    reduce_scatter x1, waiting for transfers between devices, local(): lax.psum_scatter(rounded.astype(jnp.float32).astype(jnp.bfloat16), 'row',...  239 us
    all_gather x1, waiting for transfers between devices, local(): lax.all_gather(step_low, 'row', axis=0, tiled=True)  202 us
    psum x1, blocking collectives, local(): total = lax.psum(square_total, ('row', 'col'))  39.7 us
    dot_general x1, matrix products, local(): jnp.dot(chosen, lax.all_gather(step_low, 'row', axis=0, tiled=True), pref...  23.9 us
    dot_general x1, matrix products, local(): lax.dot_general(chosen, gradient, (((0,), (0,)), ((), ())), preferred_ele...  23.2 us
    unnamed x5, local copies, waits for them, and re-layouts  21.6 us
  transfers between devices with their start and end apart: 2, of which 2 were waited for; matrix products, arithmetic and copies ran while one was open for 0% of the time, Pallas kernels for 0%

commit v1 on v0

v1 whole, which is shorter than its diff:
```python
import functools
import itertools

import jax
import jax.numpy as jnp
from jax import lax
from jax.experimental import pallas as pl
from jax.experimental.pallas import tpu as pltpu
from jax.sharding import PartitionSpec as P

MESH = pl.DeviceIdType.MESH

decay_first = 0.9
decay_second = 0.999
bias_first = 1.0 - 0.9**10
bias_second = 1.0 - 0.999**10
epsilon = 1e-08
clip_limit = 0.5

CHUNKS = 14
LEAD = 2
VMEM_BYTES = 60 * 1024 * 1024


def log2(count):
    return count.bit_length() - 1


def orders(m):
    plain = tuple(range(m))
    if m < 2:
        return plain, plain
    return plain, (1, 0) + plain[2:]


def kernel(n_row, n_col, chunks, pt_ref, g_ref, m1_ref, m2_ref, *rest):
    m, mc = log2(n_row), log2(n_col)
    gath, f_ref, s_ref, sq_ref, part, gbuf, dirv, acc, slots = rest[:9]
    recvs = rest[9 : 9 + m]
    gsem, rs_send, rs_recv, ag_send, ag_recv, loc, sq_send, sq_recv = rest[9 + m :]
    rb, w = part.shape[-2:]
    rank = pt_ref.shape[0]

    def bits_of(axis, count):
        me = lax.axis_index(axis)
        mine = [(me // (1 << b)) % 2 for b in range(count)]
        return mine, [{axis: me + (1 << b) * (1 - 2 * mine[b])} for b in range(count)]

    mine, partner = bits_of("row", m)
    _, col_partner = bits_of("col", mc)
    everyone = partner + col_partner

    def cols(c):
        return pl.ds(pl.multiple_of(c * w, w), w)

    def load(c):
        return pltpu.make_async_copy(g_ref.at[:, cols(c)], gbuf.at[c % 2], gsem.at[c % 2])

    load(0).start()
    barrier = pltpu.get_barrier_semaphore()
    for device in everyone:
        pl.semaphore_signal(barrier, inc=1, device_id=device, device_id_type=MESH)
    pl.semaphore_wait(barrier, len(everyone))
    acc[0] = jnp.zeros(acc.shape[1:], acc.dtype)

    def index(fixed):
        return tuple(fixed.get(b, slice(None)) for b in reversed(range(m)))

    def rs_copy(c, j, order):
        fixed = {b: mine[b] for b in order[:j]}
        fixed[order[j]] = 1 - mine[order[j]]
        return pltpu.make_async_remote_copy(
            src_ref=part.at[(c,) + index(fixed)],
            dst_ref=recvs[j].at[c],
            send_sem=rs_send.at[j, c],
            recv_sem=rs_recv.at[j, c],
            device_id=partner[order[j]],
            device_id_type=MESH,
        )

    def ag_copy(c, j, order):
        fixed = {b: mine[b] for b in order[: m - j]}
        view = gath.at[index(fixed) + (slice(None), cols(c))]
        return pltpu.make_async_remote_copy(
            src_ref=dirv.at[c] if j == 0 else view,
            dst_ref=view,
            send_sem=ag_send.at[j, c],
            recv_sem=ag_recv.at[j, c],
            device_id=partner[order[m - 1 - j]],
            device_id_type=MESH,
        )

    def own_copy(c):
        view = gath.at[index(dict(enumerate(mine))) + (slice(None), cols(c))]
        return pltpu.make_async_copy(dirv.at[c], view, loc.at[c])

    def project(c):
        @pl.when(c + 1 < chunks)
        def _():
            load(c + 1).start()

        load(c).wait()
        tile = min(256, rank)
        per = tile // rb

        @pl.loop(0, rank // tile)
        def _(i):
            rows = pl.ds(pl.multiple_of(i * tile, tile), tile)
            product = jnp.dot(pt_ref[rows, :], gbuf[c % 2], preferred_element_type=jnp.float32)
            product = product.astype(part.dtype)
            for k in range(per):
                owner = i * per + k
                where = tuple((owner // (1 << b)) % 2 for b in reversed(range(m)))
                part[(c,) + where] = product[k * rb : (k + 1) * rb]

    def add(c, j, order):
        fixed = {b: mine[b] for b in order[: j + 1]}
        free = [b for b in reversed(range(m)) if b not in fixed]
        for values in itertools.product(range(2), repeat=len(free)):
            at = (c,) + index({**fixed, **dict(zip(free, values))})
            arrived = recvs[j][(c,) + values].astype(jnp.float32)
            part[at] = (part[at].astype(jnp.float32) + arrived).astype(part.dtype)

    def adam(c):
        at = (c,) + index(dict(enumerate(mine)))
        step = min(32, rb)
        for r in range(0, rb, step):
            rows = pl.ds(r, step)
            low = part[at + (rows, slice(None))].astype(jnp.float32)
            low = low + recvs[m - 1][c, rows, :].astype(jnp.float32)
            first = decay_first * m1_ref[rows, cols(c)] + (1.0 - decay_first) * low
            second = decay_second * m2_ref[rows, cols(c)] + (1.0 - decay_second) * low * low
            f_ref[rows, cols(c)] = first
            s_ref[rows, cols(c)] = second
            direction = first / bias_first / (jnp.sqrt(second / bias_second) + epsilon)
            dirv[c, rows, :] = direction.astype(dirv.dtype)
            square = direction * direction
            total = square[0:8]
            for k in range(8, step, 8):
                total = total + square[k : k + 8]
            for k in range(0, w, 128):
                acc[0] += total[:, k : k + 128]

    last = 2 * m

    def step(c, s):
        for kind, order in enumerate(orders(m)):

            @pl.when((c >= 0) & (c < chunks) & ((c % 4 == 3) == (kind == 1)))
            def _():
                if 0 < s <= m:
                    rs_copy(c, s - 1, order).wait_recv()
                if s == 0:
                    project(c)
                elif s < m:
                    add(c, s - 1, order)
                elif s == m:
                    adam(c)
                    own_copy(c).start()
                else:
                    ag_copy(c, s - m - 1, order).wait_recv()
                    if s == m + 1:
                        own_copy(c).wait()
                if s < m:
                    rs_copy(c, s, order).start()
                elif s < last:
                    ag_copy(c, s - m, order).start()

    def tick(t, steps):
        for s in steps:
            step(t - (LEAD + s if s else 0), s)

    def square_copy(i):
        return pltpu.make_async_remote_copy(
            src_ref=acc.at[i],
            dst_ref=slots.at[i],
            send_sem=sq_send.at[i],
            recv_sem=sq_recv.at[i],
            device_id=everyone[i],
            device_id_type=MESH,
        )

    def square_step(i):
        square_copy(i).wait_recv()
        acc[i + 1] = acc[i] + slots[i]
        if i + 1 < len(everyone):
            square_copy(i + 1).start()

    done = chunks + LEAD + m

    @pl.loop(0, done)
    def _(t):
        tick(t, range(last, -1, -1))

    square_copy(0).start()
    at = 0
    for k in range(m):
        until = len(everyone) * (k + 1) // m
        while at < until:
            square_step(at)
            at += 1
        for s in range(last, m + k, -1):
            step(jnp.int32(done + k - LEAD - s), s)
    sq_ref[...] = acc[len(everyone)]

    for i in range(len(everyone)):
        square_copy(i).wait_send()

    @pl.loop(0, chunks)
    def _(c):
        for kind, order in enumerate(orders(m)):

            @pl.when((c % 4 == 3) == (kind == 1))
            def _():
                for j in range(m):
                    rs_copy(c, j, order).wait_send()
                    ag_copy(c, j, order).wait_send()


def local(n_row, n_col, gradient, projector, first_moment, second_moment):
    m, mc = log2(n_row), log2(n_col)
    rows, width = gradient.shape
    rank = projector.shape[1]
    rb, w = rank // n_row, width // CHUNKS
    bf16, f32 = jnp.bfloat16, jnp.float32
    pairs = (2,) * m
    whole = pl.BlockSpec(memory_space=pltpu.VMEM)
    hbm = pl.BlockSpec(memory_space=pl.ANY)
    links = m + mc
    gathered, first_new, second_new, squares = pl.pallas_call(
        functools.partial(kernel, n_row, n_col, CHUNKS),
        out_shape=[
            jax.ShapeDtypeStruct(pairs + (rb, width), bf16),
            jax.ShapeDtypeStruct((rb, width), f32),
            jax.ShapeDtypeStruct((rb, width), f32),
            jax.ShapeDtypeStruct((8, 128), f32),
        ],
        in_specs=[whole, hbm, whole, whole],
        out_specs=[hbm, whole, whole, whole],
        scratch_shapes=[
            pltpu.VMEM((CHUNKS,) + pairs + (rb, w), bf16),
            pltpu.VMEM((2, rows, w), bf16),
            pltpu.VMEM((CHUNKS, rb, w), bf16),
            pltpu.VMEM((links + 1, 8, 128), f32),
            pltpu.VMEM((links, 8, 128), f32),
        ]
        + [pltpu.VMEM((CHUNKS,) + pairs[j + 1 :] + (rb, w), bf16) for j in range(m)]
        + [pltpu.SemaphoreType.DMA((2,))]
        + [pltpu.SemaphoreType.DMA((m, CHUNKS))] * 4
        + [pltpu.SemaphoreType.DMA((CHUNKS,))]
        + [pltpu.SemaphoreType.DMA((links,))] * 2,
        cost_estimate=pl.CostEstimate(
            flops=2 * rows * rank * width,
            bytes_accessed=2 * rows * width + 2 * rank * width + 16 * rb * width,
            transcendentals=rb * width,
        ),
        compiler_params=pltpu.CompilerParams(
            collective_id=0, has_side_effects=True, vmem_limit_bytes=VMEM_BYTES
        ),
    )(projector.T, gradient, first_moment, second_moment)
    entries = rank * width * n_col
    root_mean = jnp.sqrt(jnp.sum(squares) / entries + 1e-06)
    factor = jnp.minimum(1.0, clip_limit / root_mean)
    projected = jnp.dot(
        projector, gathered.reshape(rank, width), preferred_element_type=jnp.float32
    )
    return ((projected * factor).astype(bf16), first_new, second_new)


def solution(mesh):
    placed = (P("row", "col"), P("row", None), P("row", "col"), P("row", "col"))
    return jax.shard_map(
        functools.partial(local, mesh.shape["row"], mesh.shape["col"]),
        mesh=mesh,
        in_specs=placed,
        out_specs=(P("row", "col"), P("row", "col"), P("row", "col")),
        check_vma=False,
    )
```

time: 579 us -> 390 us (0.67); the launches traced: 578 us -> 383 us
  waiting for transfers between devices: 442 us -> 0 us
  Pallas kernels: 0 us -> 324 us
  blocking collectives: 39.7 us -> 0 us
  matrix products: 47.1 us -> 24 us
  between operations: 14.7 us -> 1.34 us
  other arithmetic: 13.4 us -> 1.28 us
  local copies, waits for them, and re-layouts: 21.6 us -> 32.3 us
    pallas_call x0 -> x1, Pallas kernels: none -> 324 us  [local(): pl.pallas_call(functools.partial(kernel, n_row, n_col, CHUNKS), out_shape...]
    reduce_scatter x1 -> x0, waiting for transfers between devices: 239 us -> none  [local(): lax.psum_scatter(rounded.astype(jnp.float32).astype(jnp.bfloat16), 'row',...]
    all_gather x1 -> x0, waiting for transfers between devices: 202 us -> none  [local(): lax.all_gather(step_low, 'row', axis=0, tiled=True)]
    psum x1 -> x0, blocking collectives: 39.7 us -> none  [local(): total = lax.psum(square_total, ('row', 'col'))]
    dot_general x2 -> x1, matrix products: 47.1 us -> 24 us  [local(): jnp.dot(projector, gathered.reshape(rank, width), preferred_element_type=...]
    unnamed x5 -> x6, local copies, waits for them, and re-layouts: 21.6 us -> 32.3 us
    reduce_sum x1, other arithmetic: 7.4 us -> 1.28 us  [local(): root_mean = jnp.sqrt(jnp.sum(squares) / entries + 1e-06)]
    convert_element_type x1 -> x0, other arithmetic: 5.99 us -> none  [local(): step_low = (factor * direction).astype(jnp.bfloat16)]
  transfers between devices with their start and end apart: 2 -> 0, of which waited for: 2 -> 0; matrix products, arithmetic and copies ran while one was open for 0% -> 0% of each run, Pallas kernels for 0% -> 0%
where the time goes in v1:
time: 390 us; the launch traced here: 383 us
  Pallas kernels  324 us (83%)
  local copies, waits for them, and re-layouts  32.3 us (8%)
  matrix products  24 us (6%)
    pallas_call x1, Pallas kernels, local(): pl.pallas_call(functools.partial(kernel, n_row, n_col, CHUNKS), out_shape...  324 us
    unnamed x6, local copies, waits for them, and re-layouts  32.3 us
    dot_general x1, matrix products, local(): jnp.dot(projector, gathered.reshape(rank, width), preferred_element_type=...  24 us

profile of v1, /device:TPU:0, one launch (start us, length us, event | category | flops | bytes accessed | tf_op | source)
XLA Modules:
  0.0 383.3 jit_solution(5296915043138844651)
XLA Ops:
  0.6 3.9 %copy.7 = bf16[1024,1024]{0,1:T(8,128)(2,1)} copy(bf16[1024,1024]{1,0:T(8,128)(2,1)} %param.5) | data formatting | bytes 4194304 | tf_op args[1]
  4.6 0.0 copy-start
  4.6 324.3 %shard_map.67 = (bf16[2,2,2,128,7168]{4,3,2,1,0:T(8,128)(2,1)}, f32[128,7168]{1,0:T(8,128)}, f32[128,7168]{1,0:T(8,128)}, f32[8,128]{1,0:T(8,128)}) custom-call(bf16[1024,1024]{1,0:T(8,128)(2,1)} %bitcast.6, bf16[1024,7168]{1,0:T(8,128)(2,1)} %g_ref.1, f32[128,7168]{1,0:T(8,128)} %m1_ref.1, f32[128,7168]{1,0:T(8,128)} %m2_ref.1), custom_call_target="tpu_custom_call" | custom-call | flops 15032385536 | bytes 44040192 | tf_op jit(solution)/shard_map/pallas_call | solution.py:230
  328.9 1.3 reduce_sum.9
  330.9 0.0 copy-done
  330.9 24.0 %fusion = bf16[1024,7168]{0,1:T(8,128)(2,1)} fusion(f32[]{:T(128)S(6)} %min_shard_map.3, bf16[1024,7168]{1,0:T(8,128)(2,1)} %bitcast.7, bf16[1024,1024]{1,0:T(8,128)(2,1)S(1)} %copy-done), kind=kOutput, calls=%fused_computation.1 | convolution fusion | flops 15047065600 | bytes 31457284 | tf_op jit(solution)/shard_map/dot_general | solution.py:264
  354.9 19.9 %copy.8 = bf16[1024,7168]{1,0:T(8,128)(2,1)} copy(bf16[1024,7168]{0,1:T(8,128)(2,1)} %fusion) | data formatting | bytes 29360128
  374.8 4.2 %copy.11 = f32[128,7168]{1,0:T(8,128)} copy(f32[128,7168]{1,0:T(8,128)} %get-tuple-element.18) | data formatting | bytes 7340032
  379.0 4.2 %copy.12 = f32[128,7168]{1,0:T(8,128)} copy(f32[128,7168]{1,0:T(8,128)} %get-tuple-element.19) | data formatting | bytes 7340032
Async XLA Ops:
  4.6 326.3 %copy-start = (bf16[1024,1024]{1,0:T(8,128)(2,1)S(1)}, bf16[1024,1024]{1,0:T(8,128)(2,1)}, u32[]{:S(2)}) copy-start(bf16[1024,1024]{1,0:T(8,128)(2,1)} %param.5) | copy-start | bytes 6291460

commit v2 on v1

--- a/solution.py
+++ b/solution.py
@@ -17,9 +17,12 @@
 epsilon = 1e-08
 clip_limit = 0.5
 
-CHUNKS = 14
-LEAD = 2
+LEAD = 3
 VMEM_BYTES = 60 * 1024 * 1024
+
+
+def chunks_of(width):
+    return next(k for k in (28, 14, 8, 7, 4, 2, 1) if width % (128 * k) == 0 or k == 1)
 
 
 def log2(count):
@@ -221,14 +224,15 @@
     m, mc = log2(n_row), log2(n_col)
     rows, width = gradient.shape
     rank = projector.shape[1]
-    rb, w = rank // n_row, width // CHUNKS
+    chunks = chunks_of(width)
+    rb, w = rank // n_row, width // chunks
     bf16, f32 = jnp.bfloat16, jnp.float32
     pairs = (2,) * m
     whole = pl.BlockSpec(memory_space=pltpu.VMEM)
     hbm = pl.BlockSpec(memory_space=pl.ANY)
     links = m + mc
     gathered, first_new, second_new, squares = pl.pallas_call(
-        functools.partial(kernel, n_row, n_col, CHUNKS),
+        functools.partial(kernel, n_row, n_col, chunks),
         out_shape=[
             jax.ShapeDtypeStruct(pairs + (rb, width), bf16),
             jax.ShapeDtypeStruct((rb, width), f32),
@@ -238,16 +242,16 @@
         in_specs=[whole, hbm, whole, whole],
         out_specs=[hbm, whole, whole, whole],
         scratch_shapes=[
-            pltpu.VMEM((CHUNKS,) + pairs + (rb, w), bf16),
+            pltpu.VMEM((chunks,) + pairs + (rb, w), bf16),
             pltpu.VMEM((2, rows, w), bf16),
-            pltpu.VMEM((CHUNKS, rb, w), bf16),
+            pltpu.VMEM((chunks, rb, w), bf16),
             pltpu.VMEM((links + 1, 8, 128), f32),
             pltpu.VMEM((links, 8, 128), f32),
         ]
-        + [pltpu.VMEM((CHUNKS,) + pairs[j + 1 :] + (rb, w), bf16) for j in range(m)]
+        + [pltpu.VMEM((chunks,) + pairs[j + 1 :] + (rb, w), bf16) for j in range(m)]
         + [pltpu.SemaphoreType.DMA((2,))]
-        + [pltpu.SemaphoreType.DMA((m, CHUNKS))] * 4
-        + [pltpu.SemaphoreType.DMA((CHUNKS,))]
+        + [pltpu.SemaphoreType.DMA((m, chunks))] * 4
+        + [pltpu.SemaphoreType.DMA((chunks,))]
         + [pltpu.SemaphoreType.DMA((links,))] * 2,
         cost_estimate=pl.CostEstimate(
             flops=2 * rows * rank * width,
@@ -258,13 +262,46 @@
             collective_id=0, has_side_effects=True, vmem_limit_bytes=VMEM_BYTES
         ),
     )(projector.T, gradient, first_moment, second_moment)
-    entries = rank * width * n_col
-    root_mean = jnp.sqrt(jnp.sum(squares) / entries + 1e-06)
+    return back_project(n_col, projector, gathered.reshape(rank, width), squares, first_new, second_new)
+
+
+def back_kernel(entries, p_ref, d_ref, sq_ref, f_ref, s_ref, u_ref, fo_ref, so_ref):
+    root_mean = jnp.sqrt(jnp.sum(sq_ref[...], keepdims=True) / entries + 1e-06)
     factor = jnp.minimum(1.0, clip_limit / root_mean)
-    projected = jnp.dot(
-        projector, gathered.reshape(rank, width), preferred_element_type=jnp.float32
-    )
-    return ((projected * factor).astype(bf16), first_new, second_new)
+    rows = p_ref.shape[0]
+    tile = min(256, rows)
+    for r in range(0, rows, tile):
+        projected = jnp.dot(p_ref[r : r + tile, :], d_ref[...], preferred_element_type=jnp.float32)
+        u_ref[r : r + tile, :] = (projected * factor).astype(u_ref.dtype)
+    fo_ref[...] = f_ref[...]
+    so_ref[...] = s_ref[...]
+
+
+def back_project(n_col, projector, gathered, squares, first_new, second_new):
+    rows, rank = projector.shape
+    width = gathered.shape[1]
+    rb = first_new.shape[0]
+    steps = next(k for k in (14, 8, 7, 4, 2, 1) if width % (128 * k) == 0 or k == 1)
+    w = width // steps
+
+    def across(height):
+        return pl.BlockSpec((height, w), lambda i: (0, i))
+
+    def fixed(shape):
+        return pl.BlockSpec(shape, lambda i: (0, 0))
+
+    return pl.pallas_call(
+        functools.partial(back_kernel, rank * width * n_col),
+        grid=(steps,),
+        out_shape=[
+            jax.ShapeDtypeStruct((rows, width), jnp.bfloat16),
+            jax.ShapeDtypeStruct((rb, width), jnp.float32),
+            jax.ShapeDtypeStruct((rb, width), jnp.float32),
+        ],
+        in_specs=[fixed((rows, rank)), across(rank), fixed((8, 128)), across(rb), across(rb)],
+        out_specs=[across(rows), across(rb), across(rb)],
+        compiler_params=pltpu.CompilerParams(vmem_limit_bytes=40 * 1024 * 1024),
+    )(projector, gathered, squares, first_new, second_new)
 
 
 def solution(mesh):

time: 390 us -> 366 us (0.938); the launches traced: 383 us -> 364 us
  Pallas kernels: 324 us -> 355 us
  matrix products: 24 us -> 0 us
  local copies, waits for them, and re-layouts: 32.3 us -> 8.69 us
    pallas_call x1 -> x2, Pallas kernels: 324 us -> 355 us  [the longest x1 332 us: local(): pl.pallas_call(functools.partial(kernel, n_row, n_col, chunks), out_shape...]
    dot_general x1 -> x0, matrix products: 24 us -> none  [local(): jnp.dot(projector, gathered.reshape(rank, width), preferred_element_type=...]
    unnamed x6 -> x9, local copies, waits for them, and re-layouts: 32.3 us -> 8.69 us
where the time goes in v2:
time: 366 us; the launch traced here: 364 us
  Pallas kernels  355 us (97%)
  local copies, waits for them, and re-layouts  8.69 us (2%)
    pallas_call x1, Pallas kernels, local(): pl.pallas_call(functools.partial(kernel, n_row, n_col, chunks), out_shape...  332 us
    pallas_call x1, Pallas kernels, back_project(): pl.pallas_call(functools.partial(back_kernel, rank * width * n_col), grid...  23.4 us
    unnamed x9, local copies, waits for them, and re-layouts  8.69 us

profile of v2, /device:TPU:0, one launch (start us, length us, event | category | flops | bytes accessed | tf_op | source)
XLA Modules:
  0.0 364.3 jit_solution(17062156281818801160)
XLA Ops:
  0.6 3.9 %copy.7 = bf16[1024,1024]{0,1:T(8,128)(2,1)} copy(bf16[1024,1024]{1,0:T(8,128)(2,1)} %p_ref.1) | data formatting | bytes 4194304 | tf_op args[1]
  4.6 0.0 copy-start
  4.6 331.5 %shard_map.67 = (bf16[2,2,2,128,7168]{4,3,2,1,0:T(8,128)(2,1)}, f32[128,7168]{1,0:T(8,128)}, f32[128,7168]{1,0:T(8,128)}, f32[8,128]{1,0:T(8,128)}) custom-call(bf16[1024,1024]{1,0:T(8,128)(2,1)} %bitcast.3, bf16[1024,7168]{1,0:T(8,128)(2,1)} %g_ref.1, f32[128,7168]{1,0:T(8,128)} %m1_ref.1, f32[128,7168]{1,0:T(8,128)} %m2_ref.1), custom_call_target="tpu_custom_call" | custom-call | flops 15032385536 | bytes 44040192 | tf_op jit(solution)/shard_map/pallas_call | solution.py:234
  336.1 0.0 copy-done
  336.1 0.0 copy-start.1
  336.1 2.0 copy-done.1
  338.2 0.0 copy-start.2
  338.2 2.0 copy-done.2
  340.2 0.0 copy-start.3
  340.2 0.7 copy-done.3
  340.9 23.4 %shard_map.68 = (bf16[1024,7168]{1,0:T(8,128)(2,1)}, f32[128,7168]{1,0:T(8,128)}, f32[128,7168]{1,0:T(8,128)}) custom-call(bf16[1024,1024]{1,0:T(8,128)(2,1)S(1)} %copy-done, bf16[1024,7168]{1,0:T(8,128)(2,1)} %bitcast.2, f32[8,128]{1,0:T(8,128)S(1)} %copy-done.3, f32[128,7168]{1,0:T(8,128)S(1)} %copy-done.1, f32[128,7168]{1,0:T(8,128)S(1)} %copy-done.2), custom_call_target="tpu_custom_call" | custom-call | tf_op jit(solution)/shard_map/pallas_call | solution.py:293
Async XLA Ops:
  4.6 331.6 %copy-start = (bf16[1024,1024]{1,0:T(8,128)(2,1)S(1)}, bf16[1024,1024]{1,0:T(8,128)(2,1)}, u32[]{:S(2)}) copy-start(bf16[1024,1024]{1,0:T(8,128)(2,1)} %p_ref.1) | copy-start | bytes 6291460
  336.1 2.0 copy-start.1
  338.2 2.0 copy-start.2
  340.2 0.7 copy-start.3

commit v3 on v2

--- a/solution.py
+++ b/solution.py
@@ -17,7 +17,8 @@
 epsilon = 1e-08
 clip_limit = 0.5
 
-LEAD = 3
+LEAD = 2
+STRIDE = 2
 VMEM_BYTES = 60 * 1024 * 1024
 
 
@@ -36,13 +37,13 @@
     return plain, (1, 0) + plain[2:]
 
 
-def kernel(n_row, n_col, chunks, pt_ref, g_ref, m1_ref, m2_ref, *rest):
+def kernel(n_row, n_col, chunks, p_ref, g_ref, m1_ref, m2_ref, *rest):
     m, mc = log2(n_row), log2(n_col)
-    gath, f_ref, s_ref, sq_ref, part, gbuf, dirv, acc, slots = rest[:9]
-    recvs = rest[9 : 9 + m]
-    gsem, rs_send, rs_recv, ag_send, ag_recv, loc, sq_send, sq_recv = rest[9 + m :]
+    gath, f_ref, s_ref, sq_ref, u_ref, part, gbuf, dirv, acc, slots, pt_ref, dbuf, ubuf = rest[:13]
+    recvs = rest[13 : 13 + m]
+    gsem, dsem, usem, rs_send, rs_recv, ag_send, ag_recv, loc, sq_send, sq_recv = rest[13 + m :]
     rb, w = part.shape[-2:]
-    rank = pt_ref.shape[0]
+    rows_here, rank = p_ref.shape
 
     def bits_of(axis, count):
         me = lax.axis_index(axis)
@@ -60,6 +61,8 @@
         return pltpu.make_async_copy(g_ref.at[:, cols(c)], gbuf.at[c % 2], gsem.at[c % 2])
 
     load(0).start()
+    for r in range(0, rank, min(256, rank)):
+        pt_ref[r : r + min(256, rank), :] = p_ref[:, r : r + min(256, rank)].T
     barrier = pltpu.get_barrier_semaphore()
     for device in everyone:
         pl.semaphore_signal(barrier, inc=1, device_id=device, device_id_type=MESH)
@@ -144,9 +147,49 @@
             for k in range(0, w, 128):
                 acc[0] += total[:, k : k + 128]
 
+    def gathered_load(c):
+        return pltpu.make_async_copy(
+            gath.at[(slice(None),) * (m + 1) + (cols(c),)], dbuf.at[c % 2], dsem.at[c % 2]
+        )
+
+    def update_store(c):
+        return pltpu.make_async_copy(ubuf.at[c % 2], u_ref.at[:, cols(c)], usem.at[c % 2])
+
+    def back(c):
+        gathered_load(c).wait()
+
+        @pl.when(c >= 2)
+        def _():
+            update_store(c - 2).wait()
+
+        tile = min(256, rows_here)
+        direction = dbuf.at[c % 2]
+
+        @pl.loop(0, rows_here // tile)
+        def _(i):
+            rows = pl.ds(pl.multiple_of(i * tile, tile), tile)
+            product = jnp.dot(
+                p_ref[rows, :],
+                direction[...].reshape(rank, w),
+                preferred_element_type=jnp.float32,
+            )
+            ubuf[c % 2, rows, :] = product.astype(ubuf.dtype)
+
+        update_store(c).start()
+
     last = 2 * m
+    lags = [0] + [LEAD + STRIDE * s for s in range(1, last + 1)]
+    lags.append(lags[last] + 1)
+    turn = list(range(last, 0, -1)) + [last + 1, 0]
 
     def step(c, s):
+        if s == last + 1:
+
+            @pl.when((c >= 0) & (c < chunks))
+            def _():
+                back(c)
+
+            return
         for kind, order in enumerate(orders(m)):
 
             @pl.when((c >= 0) & (c < chunks) & ((c % 4 == 3) == (kind == 1)))
@@ -164,14 +207,12 @@
                     ag_copy(c, s - m - 1, order).wait_recv()
                     if s == m + 1:
                         own_copy(c).wait()
+                    if s == last:
+                        gathered_load(c).start()
                 if s < m:
                     rs_copy(c, s, order).start()
                 elif s < last:
                     ag_copy(c, s - m, order).start()
-
-    def tick(t, steps):
-        for s in steps:
-            step(t - (LEAD + s if s else 0), s)
 
     def square_copy(i):
         return pltpu.make_async_remote_copy(
@@ -189,21 +230,29 @@
         if i + 1 < len(everyone):
             square_copy(i + 1).start()
 
-    done = chunks + LEAD + m
+    done = chunks + lags[m]
 
     @pl.loop(0, done)
     def _(t):
-        tick(t, range(last, -1, -1))
+        for s in turn:
+            step(t - lags[s], s)
 
     square_copy(0).start()
-    at = 0
-    for k in range(m):
-        until = len(everyone) * (k + 1) // m
-        while at < until:
-            square_step(at)
-            at += 1
-        for s in range(last, m + k, -1):
-            step(jnp.int32(done + k - LEAD - s), s)
+    for i in range(len(everyone)):
+        square_step(i)
+        if i < m:
+            for s in turn:
+                if s > m:
+                    step(jnp.int32(done + i - lags[s]), s)
+
+    @pl.loop(done + min(m, len(everyone)), chunks + lags[last + 1])
+    def _(t):
+        for s in turn:
+            if s > m:
+                step(t - lags[s], s)
+
+    for c in range(max(chunks - 2, 0), chunks):
+        update_store(c).wait()
     sq_ref[...] = acc[len(everyone)]
 
     for i in range(len(everyone)):
@@ -231,77 +280,72 @@
     whole = pl.BlockSpec(memory_space=pltpu.VMEM)
     hbm = pl.BlockSpec(memory_space=pl.ANY)
     links = m + mc
-    gathered, first_new, second_new, squares = pl.pallas_call(
+    _, first_new, second_new, squares, unscaled = pl.pallas_call(
         functools.partial(kernel, n_row, n_col, chunks),
         out_shape=[
             jax.ShapeDtypeStruct(pairs + (rb, width), bf16),
             jax.ShapeDtypeStruct((rb, width), f32),
             jax.ShapeDtypeStruct((rb, width), f32),
             jax.ShapeDtypeStruct((8, 128), f32),
+            jax.ShapeDtypeStruct((rows, width), bf16),
         ],
         in_specs=[whole, hbm, whole, whole],
-        out_specs=[hbm, whole, whole, whole],
+        out_specs=[hbm, whole, whole, whole, hbm],
         scratch_shapes=[
             pltpu.VMEM((chunks,) + pairs + (rb, w), bf16),
             pltpu.VMEM((2, rows, w), bf16),
             pltpu.VMEM((chunks, rb, w), bf16),
             pltpu.VMEM((links + 1, 8, 128), f32),
             pltpu.VMEM((links, 8, 128), f32),
+            pltpu.VMEM((rank, rows), bf16),
+            pltpu.VMEM((2,) + pairs + (rb, w), bf16),
+            pltpu.VMEM((2, rows, w), bf16),
         ]
         + [pltpu.VMEM((chunks,) + pairs[j + 1 :] + (rb, w), bf16) for j in range(m)]
-        + [pltpu.SemaphoreType.DMA((2,))]
+        + [pltpu.SemaphoreType.DMA((2,))] * 3
         + [pltpu.SemaphoreType.DMA((m, chunks))] * 4
         + [pltpu.SemaphoreType.DMA((chunks,))]
         + [pltpu.SemaphoreType.DMA((links,))] * 2,
         cost_estimate=pl.CostEstimate(
-            flops=2 * rows * rank * width,
+            flops=4 * rows * rank * width,
             bytes_accessed=2 * rows * width + 2 * rank * width + 16 * rb * width,
             transcendentals=rb * width,
         ),
         compiler_params=pltpu.CompilerParams(
             collective_id=0, has_side_effects=True, vmem_limit_bytes=VMEM_BYTES
         ),
-    )(projector.T, gradient, first_moment, second_moment)
-    return back_project(n_col, projector, gathered.reshape(rank, width), squares, first_new, second_new)
-
-
-def back_kernel(entries, p_ref, d_ref, sq_ref, f_ref, s_ref, u_ref, fo_ref, so_ref):
+    )(projector, gradient, first_moment, second_moment)
+    return scale(rank * width * n_col, unscaled, squares, first_new, second_new)
+
+
+def scale_kernel(entries, v_ref, sq_ref, f_ref, s_ref, u_ref, fo_ref, so_ref):
     root_mean = jnp.sqrt(jnp.sum(sq_ref[...], keepdims=True) / entries + 1e-06)
     factor = jnp.minimum(1.0, clip_limit / root_mean)
-    rows = p_ref.shape[0]
-    tile = min(256, rows)
-    for r in range(0, rows, tile):
-        projected = jnp.dot(p_ref[r : r + tile, :], d_ref[...], preferred_element_type=jnp.float32)
-        u_ref[r : r + tile, :] = (projected * factor).astype(u_ref.dtype)
+    u_ref[...] = (v_ref[...].astype(jnp.float32) * factor).astype(u_ref.dtype)
     fo_ref[...] = f_ref[...]
     so_ref[...] = s_ref[...]
 
 
-def back_project(n_col, projector, gathered, squares, first_new, second_new):
-    rows, rank = projector.shape
-    width = gathered.shape[1]
+def scale(entries, unscaled, squares, first_new, second_new):
+    rows, width = unscaled.shape
     rb = first_new.shape[0]
-    steps = next(k for k in (14, 8, 7, 4, 2, 1) if width % (128 * k) == 0 or k == 1)
-    w = width // steps
-
-    def across(height):
-        return pl.BlockSpec((height, w), lambda i: (0, i))
-
-    def fixed(shape):
-        return pl.BlockSpec(shape, lambda i: (0, 0))
+    steps = next(k for k in (8, 4, 2, 1) if rows % (16 * k) == 0 and rb % (8 * k) == 0 or k == 1)
+
+    def down(height):
+        return pl.BlockSpec((height // steps, width), lambda i: (i, 0))
 
     return pl.pallas_call(
-        functools.partial(back_kernel, rank * width * n_col),
+        functools.partial(scale_kernel, entries),
         grid=(steps,),
         out_shape=[
             jax.ShapeDtypeStruct((rows, width), jnp.bfloat16),
             jax.ShapeDtypeStruct((rb, width), jnp.float32),
             jax.ShapeDtypeStruct((rb, width), jnp.float32),
         ],
-        in_specs=[fixed((rows, rank)), across(rank), fixed((8, 128)), across(rb), across(rb)],
-        out_specs=[across(rows), across(rb), across(rb)],
-        compiler_params=pltpu.CompilerParams(vmem_limit_bytes=40 * 1024 * 1024),
-    )(projector, gathered, squares, first_new, second_new)
+        in_specs=[down(rows), pl.BlockSpec((8, 128), lambda i: (0, 0)), down(rb), down(rb)],
+        out_specs=[down(rows), down(rb), down(rb)],
+        compiler_params=pltpu.CompilerParams(vmem_limit_bytes=VMEM_BYTES),
+    )(unscaled, squares, first_new, second_new)
 
 
 def solution(mesh):

time: 366 us -> 334 us (0.913)
  Pallas kernels: 355 us -> 333 us
  local copies, waits for them, and re-layouts: 8.69 us -> 0 us
    pallas_call x1, Pallas kernels: 332 us -> 316 us  [local(): pl.pallas_call(functools.partial(kernel, n_row, n_col, chunks), out_shape...]
    unnamed x9 -> x0, local copies, waits for them, and re-layouts: 8.69 us -> none
    pallas_call x1, Pallas kernels: 23.4 us -> 17 us  [scale(): pl.pallas_call(functools.partial(scale_kernel, entries), grid=(steps,), o...]
where the time goes in v3:
time: 334 us
  Pallas kernels  333 us (100%)
    pallas_call x1, Pallas kernels, local(): pl.pallas_call(functools.partial(kernel, n_row, n_col, chunks), out_shape...  316 us
    pallas_call x1, Pallas kernels, scale(): pl.pallas_call(functools.partial(scale_kernel, entries), grid=(steps,), o...  17 us

profile of v3, /device:TPU:0, one launch (start us, length us, event | category | flops | bytes accessed | tf_op | source)
XLA Modules:
  0.0 334.1 jit_solution(14008164475189779308)
XLA Ops:
  0.6 316.4 %shard_map.67 = (bf16[2,2,2,128,7168]{4,3,2,1,0:T(8,128)(2,1)}, f32[128,7168]{1,0:T(8,128)}, f32[128,7168]{1,0:T(8,128)}, f32[8,128]{1,0:T(8,128)}, bf16[1024,7168]{1,0:T(8,128)(2,1)}) custom-call(bf16[1024,1024]{1,0:T(8,128)(2,1)} %p_ref.1, bf16[1024,7168]{1,0:T(8,128)(2,1)} %g_ref.1, f32[128,7168]{1,0:T(8,128)} %m1_ref.1, f32[128,7168]{1,0:T(8,128)} %m2_ref.1), custom_call_target="tpu_custom_call" | custom-call | flops 30064771072 | bytes 44040192 | tf_op jit(solution)/shard_map/pallas_call | solution.py:283
  317.1 17.0 %shard_map.68 = (bf16[1024,7168]{1,0:T(8,128)(2,1)}, f32[128,7168]{1,0:T(8,128)}, f32[128,7168]{1,0:T(8,128)}) custom-call(bf16[1024,7168]{1,0:T(8,128)(2,1)} %get-tuple-element.7.v_ref, f32[8,128]{1,0:T(8,128)} %get-tuple-element.8.sq_ref, f32[128,7168]{1,0:T(8,128)} %get-tuple-element.9.f_ref, f32[128,7168]{1,0:T(8,128)} %get-tuple-element.10.s_ref), custom_call_target="tpu_custom_call" | custom-call | tf_op jit(solution)/shard_map/pallas_call | solution.py:337

commit v4 on v3

--- a/solution.py
+++ b/solution.py
@@ -18,7 +18,7 @@
 clip_limit = 0.5
 
 LEAD = 2
-STRIDE = 2
+STRIDE = 3
 VMEM_BYTES = 60 * 1024 * 1024
 
 
@@ -37,11 +37,13 @@
     return plain, (1, 0) + plain[2:]
 
 
-def kernel(n_row, n_col, chunks, p_ref, g_ref, m1_ref, m2_ref, *rest):
+def kernel(n_row, n_col, chunks, p_ref, g_ref, m1_hbm, m2_hbm, *rest):
     m, mc = log2(n_row), log2(n_col)
-    gath, f_ref, s_ref, sq_ref, u_ref, part, gbuf, dirv, acc, slots, pt_ref, dbuf, ubuf = rest[:13]
-    recvs = rest[13 : 13 + m]
-    gsem, dsem, usem, rs_send, rs_recv, ag_send, ag_recv, loc, sq_send, sq_recv = rest[13 + m :]
+    gath, f_hbm, s_hbm, sq_ref, u_ref, part, gbuf, dirv, acc, slots, pt_ref, dbuf, ubuf = rest[:13]
+    m1_ref, m2_ref, f_ref, s_ref = rest[13:17]
+    recvs = rest[17 : 17 + m]
+    gsem, dsem, usem, msem, fsem, rs_send, rs_recv = rest[17 + m : 24 + m]
+    ag_send, ag_recv, loc, sq_send, sq_recv = rest[24 + m :]
     rb, w = part.shape[-2:]
     rows_here, rank = p_ref.shape
 
@@ -60,13 +62,21 @@
     def load(c):
         return pltpu.make_async_copy(g_ref.at[:, cols(c)], gbuf.at[c % 2], gsem.at[c % 2])
 
-    load(0).start()
-    for r in range(0, rank, min(256, rank)):
-        pt_ref[r : r + min(256, rank), :] = p_ref[:, r : r + min(256, rank)].T
     barrier = pltpu.get_barrier_semaphore()
     for device in everyone:
         pl.semaphore_signal(barrier, inc=1, device_id=device, device_id_type=MESH)
+    load(0).start()
+    moments = [
+        pltpu.make_async_copy(m1_hbm, m1_ref, msem.at[0]),
+        pltpu.make_async_copy(m2_hbm, m2_ref, msem.at[1]),
+    ]
+    for copy in moments:
+        copy.start()
+    for r in range(0, rank, min(256, rank)):
+        pt_ref[r : r + min(256, rank), :] = p_ref[:, r : r + min(256, rank)].T
     pl.semaphore_wait(barrier, len(everyone))
+    for copy in moments:
+        copy.wait()
     acc[0] = jnp.zeros(acc.shape[1:], acc.dtype)
 
     def index(fixed):
@@ -86,7 +96,7 @@
 
     def ag_copy(c, j, order):
         fixed = {b: mine[b] for b in order[: m - j]}
-        view = gath.at[index(fixed) + (slice(None), cols(c))]
+        view = gath.at[(c,) + index(fixed)]
         return pltpu.make_async_remote_copy(
             src_ref=dirv.at[c] if j == 0 else view,
             dst_ref=view,
@@ -97,7 +107,7 @@
         )
 
     def own_copy(c):
-        view = gath.at[index(dict(enumerate(mine))) + (slice(None), cols(c))]
+        view = gath.at[(c,) + index(dict(enumerate(mine)))]
         return pltpu.make_async_copy(dirv.at[c], view, loc.at[c])
 
     def project(c):
@@ -148,9 +158,13 @@
                 acc[0] += total[:, k : k + 128]
 
     def gathered_load(c):
-        return pltpu.make_async_copy(
-            gath.at[(slice(None),) * (m + 1) + (cols(c),)], dbuf.at[c % 2], dsem.at[c % 2]
-        )
+        return pltpu.make_async_copy(gath.at[c], dbuf.at[c % 2], dsem.at[c % 2])
+
+    def moment_stores(c):
+        return [
+            pltpu.make_async_copy(f_ref.at[:, cols(c)], f_hbm.at[:, cols(c)], fsem.at[0, c]),
+            pltpu.make_async_copy(s_ref.at[:, cols(c)], s_hbm.at[:, cols(c)], fsem.at[1, c]),
+        ]
 
     def update_store(c):
         return pltpu.make_async_copy(ubuf.at[c % 2], u_ref.at[:, cols(c)], usem.at[c % 2])
@@ -203,6 +217,8 @@
                 elif s == m:
                     adam(c)
                     own_copy(c).start()
+                    for copy in moment_stores(c):
+                        copy.start()
                 else:
                     ag_copy(c, s - m - 1, order).wait_recv()
                     if s == m + 1:
@@ -260,6 +276,8 @@
 
     @pl.loop(0, chunks)
     def _(c):
+        for copy in moment_stores(c):
+            copy.wait()
         for kind, order in enumerate(orders(m)):
 
             @pl.when((c % 4 == 3) == (kind == 1))
@@ -283,14 +301,14 @@
     _, first_new, second_new, squares, unscaled = pl.pallas_call(
         functools.partial(kernel, n_row, n_col, chunks),
         out_shape=[
-            jax.ShapeDtypeStruct(pairs + (rb, width), bf16),
+            jax.ShapeDtypeStruct((chunks,) + pairs + (rb, w), bf16),
             jax.ShapeDtypeStruct((rb, width), f32),
             jax.ShapeDtypeStruct((rb, width), f32),
             jax.ShapeDtypeStruct((8, 128), f32),
             jax.ShapeDtypeStruct((rows, width), bf16),
         ],
-        in_specs=[whole, hbm, whole, whole],
-        out_specs=[hbm, whole, whole, whole, hbm],
+        in_specs=[whole, hbm, hbm, hbm],
+        out_specs=[hbm, hbm, hbm, whole, hbm],
         scratch_shapes=[
             pltpu.VMEM((chunks,) + pairs + (rb, w), bf16),
             pltpu.VMEM((2, rows, w), bf16),
@@ -301,8 +319,10 @@
             pltpu.VMEM((2,) + pairs + (rb, w), bf16),
             pltpu.VMEM((2, rows, w), bf16),
         ]
+        + [pltpu.VMEM((rb, width), f32)] * 4
         + [pltpu.VMEM((chunks,) + pairs[j + 1 :] + (rb, w), bf16) for j in range(m)]
-        + [pltpu.SemaphoreType.DMA((2,))] * 3
+        + [pltpu.SemaphoreType.DMA((2,))] * 4
+        + [pltpu.SemaphoreType.DMA((2, chunks))]
         + [pltpu.SemaphoreType.DMA((m, chunks))] * 4
         + [pltpu.SemaphoreType.DMA((chunks,))]
         + [pltpu.SemaphoreType.DMA((links,))] * 2,

time: 334 us -> 329 us (0.985)
  Pallas kernels: 333 us -> 329 us
    pallas_call x1, Pallas kernels: 316 us -> 312 us  [local(): pl.pallas_call(functools.partial(kernel, n_row, n_col, chunks), out_shape...]
where the time goes in v4:
time: 329 us
  Pallas kernels  329 us (100%)
    pallas_call x1, Pallas kernels, local(): pl.pallas_call(functools.partial(kernel, n_row, n_col, chunks), out_shape...  312 us
    pallas_call x1, Pallas kernels, scale(): pl.pallas_call(functools.partial(scale_kernel, entries), grid=(steps,), o...  17 us

profile of v4, /device:TPU:0, one launch (start us, length us, event | category | flops | bytes accessed | tf_op | source)
XLA Modules:
  0.0 329.2 jit_solution(16163201499165890709)
XLA Ops:
  0.6 311.6 %shard_map.67 = (bf16[28,2,2,2,128,256]{5,4,3,2,1,0:T(8,128)(2,1)}, f32[128,7168]{1,0:T(8,128)}, f32[128,7168]{1,0:T(8,128)}, f32[8,128]{1,0:T(8,128)}, bf16[1024,7168]{1,0:T(8,128)(2,1)}) custom-call(bf16[1024,1024]{1,0:T(8,128)(2,1)} %p_ref.1, bf16[1024,7168]{1,0:T(8,128)(2,1)} %g_ref.1, f32[128,7168]{1,0:T(8,128)} %m1_hbm.1, f32[128,7168]{1,0:T(8,128)} %m2_hbm.1), custom_call_target="tpu_custom_call" | custom-call | flops 30064771072 | bytes 44040192 | tf_op jit(solution)/shard_map/pallas_call | solution.py:301
  312.2 17.0 %shard_map.68 = (bf16[1024,7168]{1,0:T(8,128)(2,1)}, f32[128,7168]{1,0:T(8,128)}, f32[128,7168]{1,0:T(8,128)}) custom-call(bf16[1024,7168]{1,0:T(8,128)(2,1)} %get-tuple-element.7.v_ref, f32[8,128]{1,0:T(8,128)} %get-tuple-element.8.sq_ref, f32[128,7168]{1,0:T(8,128)} %get-tuple-element.9.f_ref, f32[128,7168]{1,0:T(8,128)} %get-tuple-element.10.s_ref), custom_call_target="tpu_custom_call" | custom-call | tf_op jit(solution)/shard_map/pallas_call | solution.py:357

commit v5 on v4

--- a/solution.py
+++ b/solution.py
@@ -206,7 +206,7 @@
             return
         for kind, order in enumerate(orders(m)):
 
-            @pl.when((c >= 0) & (c < chunks) & ((c % 4 == 3) == (kind == 1)))
+            @pl.when((c >= 0) & (c < chunks) & ((c % 7 == 6) == (kind == 1)))
             def _():
                 if 0 < s <= m:
                     rs_copy(c, s - 1, order).wait_recv()
@@ -280,7 +280,7 @@
             copy.wait()
         for kind, order in enumerate(orders(m)):
 
-            @pl.when((c % 4 == 3) == (kind == 1))
+            @pl.when((c % 7 == 6) == (kind == 1))
             def _():
                 for j in range(m):
                     rs_copy(c, j, order).wait_send()

time: 329 us -> 331 us (level)
  no operation moved by 1% of the time
where the time goes in v5:
time: 331 us
  Pallas kernels  331 us (100%)
    pallas_call x1, Pallas kernels, local(): pl.pallas_call(functools.partial(kernel, n_row, n_col, chunks), out_shape...  313 us
    pallas_call x1, Pallas kernels, scale(): pl.pallas_call(functools.partial(scale_kernel, entries), grid=(steps,), o...  17 us

profile of v5, /device:TPU:0, one launch (start us, length us, event | category | flops | bytes accessed | tf_op | source)
XLA Modules:
  0.0 331.2 jit_solution(4161924154998659442)
XLA Ops:
  0.6 313.5 %shard_map.67 = (bf16[28,2,2,2,128,256]{5,4,3,2,1,0:T(8,128)(2,1)}, f32[128,7168]{1,0:T(8,128)}, f32[128,7168]{1,0:T(8,128)}, f32[8,128]{1,0:T(8,128)}, bf16[1024,7168]{1,0:T(8,128)(2,1)}) custom-call(bf16[1024,1024]{1,0:T(8,128)(2,1)} %p_ref.1, bf16[1024,7168]{1,0:T(8,128)(2,1)} %g_ref.1, f32[128,7168]{1,0:T(8,128)} %m1_hbm.1, f32[128,7168]{1,0:T(8,128)} %m2_hbm.1), custom_call_target="tpu_custom_call" | custom-call | flops 30064771072 | bytes 44040192 | tf_op jit(solution)/shard_map/pallas_call | solution.py:301
  314.1 17.0 %shard_map.68 = (bf16[1024,7168]{1,0:T(8,128)(2,1)}, f32[128,7168]{1,0:T(8,128)}, f32[128,7168]{1,0:T(8,128)}) custom-call(bf16[1024,7168]{1,0:T(8,128)(2,1)} %get-tuple-element.7.v_ref, f32[8,128]{1,0:T(8,128)} %get-tuple-element.8.sq_ref, f32[128,7168]{1,0:T(8,128)} %get-tuple-element.9.f_ref, f32[128,7168]{1,0:T(8,128)} %get-tuple-element.10.s_ref), custom_call_target="tpu_custom_call" | custom-call | tf_op jit(solution)/shard_map/pallas_call | solution.py:357
